TPU v7x, 256 devices: a whole 4x4x8 slice. The times are simulated.
256 devices in a mesh: ra: 16 (over x, z_hi, core), rb: 16 (over y, z_lo).
Axes of the slice: x: 4, y: 4, z: 8 (z_hi: 2, z_lo: 4; z = z_hi * 4 + z_lo), core: 2. Of those that a mesh axis runs over, the one named last changes fastest.
Arguments:
- features_a: bfloat16 [32, 128, 1024], P('ra', 'rb'), may hold values from -600 to 600
- features_b: bfloat16 [32, 128, 1024], P('rb', 'ra'), may hold values from -600 to 600
- weight_one: bfloat16 [16, 81], replicated, may hold values from -16 to 16
- bias_one: float32 [16], replicated, may hold values from -3 to 3
- weight_two: bfloat16 [16, 81], replicated, may hold values from -0.25 to 0.25
- bias_two: float32 [1], replicated, may hold values from -3 to 3
Outputs:
- consensus: float32 [32, 128, 32, 128], P('ra', None, 'rb')
All inputs are finite; a program needn't handle non-finite values.
Results may differ from a plain program's by a relative error of at most 0.0053.
Values may be sent and summed in bfloat16 or wider, within the bound.
A program may use at most 192 MiB of HBM per device.

v0:
```python
import jax
import jax.numpy as jnp
from jax import lax
from jax.sharding import PartitionSpec as P


def extended(cells, sides, width):
    for axis, dim in sides:
        count = lax.axis_size(axis)
        ends = count - 1
        head = lax.slice_in_dim(cells, 0, width, axis=dim)
        tail = lax.slice_in_dim(cells, cells.shape[dim] - width, cells.shape[dim], axis=dim)
        cells = jnp.concatenate(
            [
                lax.ppermute(tail, axis, [(i, (i + 1) % count) for i in range(ends)]),
                cells,
                lax.ppermute(head, axis, [((i + 1) % count, i) for i in range(ends)]),
            ],
            axis=dim,
        )
    return cells


def normalize(features):
    values = features.astype(jnp.float32)
    scale = lax.rsqrt(jnp.sum(values * values, axis=-1, keepdims=True) + 1e-06)
    return (values * scale).astype(jnp.bfloat16)


def correlate(norm_a, norm_b):
    gathered = lax.all_gather(norm_a, "rb", axis=1, tiled=True)
    channels = gathered.shape[2]
    flat_a = gathered.reshape(-1, channels)
    piece = lax.all_gather(norm_b, "ra", axis=1, tiled=True)
    product = lax.dot_general(
        flat_a,
        piece.reshape(-1, channels),
        (((1,), (1,)), ((), ())),
        preferred_element_type=jnp.float32,
    )
    return product.reshape(
        gathered.shape[0], gathered.shape[1], piece.shape[0], piece.shape[1]
    ).astype(jnp.bfloat16)


def pad_columns(volume):
    return jnp.pad(volume, ((0, 0), (1, 1), (0, 0), (1, 1)))


def first_layer(volume, weight_one, bias_one, out_rows, out_k):
    width_j = volume.shape[1] - 2
    width_l = volume.shape[3] - 2

    def first_one_row(row_start):
        block = lax.dynamic_slice_in_dim(volume, row_start, 3, 0)
        patches = jnp.stack(
            [
                block[t_i, t_j : t_j + width_j, t_k : t_k + out_k, t_l : t_l + width_l]
                for t_i in range(3)
                for t_j in range(3)
                for t_k in range(3)
                for t_l in range(3)
            ]
        )
        before = lax.dot_general(
            weight_one, patches, (((1,), (0,)), ((), ())), preferred_element_type=jnp.float32
        )
        return jax.nn.relu(before + bias_one[:, None, None, None])

    return lax.map(first_one_row, jnp.arange(out_rows, dtype=jnp.int32))


def second_sums(hidden_pad, weight_two, out_rows, out_k):
    width_j = hidden_pad.shape[2] - 2
    width_l = hidden_pad.shape[4] - 2

    def second_one_row(row_start):
        total = jnp.zeros((width_j, out_k, width_l), jnp.float32)
        for t_i in range(3):
            plane = lax.dynamic_index_in_dim(hidden_pad, row_start + t_i, 0, keepdims=False)
            taps = lax.dot_general(
                weight_two[:, 27 * t_i : 27 * t_i + 27],
                plane,
                (((0,), (0,)), ((), ())),
                preferred_element_type=jnp.float32,
            )
            for t_j in range(3):
                for t_k in range(3):
                    for t_l in range(3):
                        total = (
                            total
                            + taps[
                                9 * t_j + 3 * t_k + t_l,
                                t_j : t_j + width_j,
                                t_k : t_k + out_k,
                                t_l : t_l + width_l,
                            ]
                        )
        return total

    return lax.map(second_one_row, jnp.arange(out_rows, dtype=jnp.int32))


def second_layer(hidden_pad, weight_two, bias_two, out_rows, out_k):
    return jax.nn.relu(second_sums(hidden_pad, weight_two, out_rows, out_k) + bias_two[0])


def per_device(features_a, features_b, weight_one, bias_one, weight_two, bias_two):
    norm_a = normalize(features_a)
    norm_b = normalize(features_b)
    rows_a = norm_a.shape[0]
    rows_b = norm_b.shape[0]
    volume = correlate(norm_a, norm_b)
    padded = extended(volume, (("ra", 0), ("rb", 2)), 1)
    hidden = first_layer(pad_columns(padded), weight_one, bias_one, rows_a, rows_b).astype(
        jnp.bfloat16
    )
    hidden = extended(hidden, (("ra", 0), ("rb", 3)), 1)
    hidden = jnp.pad(hidden, ((0, 0), (0, 0), (1, 1), (0, 0), (1, 1)))
    return second_layer(hidden, weight_two, bias_two, rows_a, rows_b)


def solution(mesh):
    return jax.shard_map(
        per_device,
        mesh=mesh,
        in_specs=(P("ra", "rb", None), P("rb", "ra", None), P(), P(), P(), P()),
        out_specs=P("ra", None, "rb", None),
        check_vma=False,
    )
```

profile of v0, /device:TPU:232, one launch (start us, length us, event | category | flops | bytes accessed | tf_op | source)
XLA Modules:
  0.0 701.4 jit_solution(13057398529258511894)
XLA Ops:
  1.7 36.8 %all_gather.6 = bf16[2,128,1024]{2,1,0:T(8,128)(2,1)S(1)} all-gather(bf16[2,8,1024]{2,1,0:T(8,128)(2,1)S(1)} %fusion.41), channel_id=1, replica_groups=mesh['ra'=16,'rb'=16] {'rb'}, dimensions={1}, use_global_device_ids=true | all-gather | bytes 557056 | tf_op jit(solution)/shard_map/all_gather | solution.py:31
  40.2 27.3 %all_gather.7 = bf16[2,128,1024]{2,1,0:T(8,128)(2,1)S(1)} all-gather(bf16[2,8,1024]{2,1,0:T(8,128)(2,1)S(1)} %fusion.43), channel_id=1, replica_groups=mesh['ra'=16,'rb'=16] {'ra'}, dimensions={1}, use_global_device_ids=true | all-gather | bytes 557056 | tf_op jit(solution)/shard_map/all_gather | solution.py:34
  70.2 9.7 %collective-permute-start.1 = (bf16[1,128,2,128]{3,1,2,0:T(8,128)(2,1)S(1)}, bf16[1,128,2,128]{3,1,2,0:T(8,128)(2,1)S(1)}, u32[]{:S(2)}, u32[]{:S(2)}) collective-permute-start(bf16[1,128,2,128]{3,1,2,0:T(8,128)(2,1)S(1)} %get-tuple-element.226), channel_id=1, source_target_pairs={{16,0},{32,16},{48,32},{64,48},{80,64},{96,80},{112,96},{128,112},... | collective-permute-start | bytes 196616 | tf_op jit(solution)/shard_map/ppermute | solution.py:17
  81.8 5.7 collective-permute-start.2
  90.6 7.8 %collective-permute-done.3 = bf16[4,128,1,128]{3,1,2,0:T(8,128)(2,1)} collective-permute-done((bf16[4,128,1,128]{3,1,2,0:T(8,128)(2,1)S(1)}, bf16[4,128,1,128]{3,1,2,0:T(8,128)(2,1)}, u32[]{:S(2)}, u32[]{:S(2)}) %collective-permute-start.3) | collective-permute-done | bytes 131104 | tf_op jit(solution)/shard_map/ppermute | solution.py:17
  100.3 225.3 %while.24 = (s32[]{:T(128)}, bf16[2,16,128,2,128]{4,1,3,2,0:T(8,128)(2,1)S(1)}, s32[2]{0:T(128)S(1)}, bf16[4,130,4,130]{3,1,2,0:T(8,128)(2,1)S(1)}, bf16[16,81]{1,0:T(8,128)(2,1)S(1)}, /*index=5*/f32[16]{0:T(128)S(1)}) while((s32[]{:T(128)}, bf16[2,16,128,2,128]{4,1,3,2,0:T(8,128)(2,1)S(1)}, s32[2]{0:T(128)S(1)}, ...), condition=%wide.region_3.4_spmd.clone, body=%wide.region_2.3_spmd.sunk.clone | while | flops 85983240 | bytes 39260856 | solution.py:70
  167.6 41.6 %stack.5 = bf16[81,128,2,128]{3,0,2,1:T(8,128)(2,1)} concatenate(bf16[1,128,2,128]{3,0,2,1:T(2,128)(2,1)S(1)} %copy.263, bf16[1,128,2,128]{3,0,2,1:T(2,128)(2,1)S(1)} %copy.264, bf16[1,128,2,128]{3,0,2,1:T(2,128)(2,1)} %copy.265, bf16[1,128,2,128]{3,0,2,1:T(2,128)(2,1)} %copy.266, bf16[1,128,2,128]{3,0,2,1:T(2,128)(2,1)} %copy.267, bf16[1,128,2,128]{3,0,2,1:T(2,128)(2,1)} %copy.268, ...), dimensions={0} | concatenate | bytes 10616832 | tf_op jit(solution)/shard_map/while/body/eval_jaxpr/stack | solution.py:56
  280.2 41.6 %stack.5 = bf16[81,128,2,128]{3,0,2,1:T(8,128)(2,1)} concatenate(bf16[1,128,2,128]{3,0,2,1:T(2,128)(2,1)S(1)} %copy.263, bf16[1,128,2,128]{3,0,2,1:T(2,128)(2,1)S(1)} %copy.264, bf16[1,128,2,128]{3,0,2,1:T(2,128)(2,1)} %copy.265, bf16[1,128,2,128]{3,0,2,1:T(2,128)(2,1)} %copy.266, bf16[1,128,2,128]{3,0,2,1:T(2,128)(2,1)} %copy.267, bf16[1,128,2,128]{3,0,2,1:T(2,128)(2,1)} %copy.268, ...), dimensions={0} | concatenate | bytes 10616832 | tf_op jit(solution)/shard_map/while/body/eval_jaxpr/stack | solution.py:56
  329.8 5.7 collective-permute-start.5
  335.5 28.8 %collective-permute-done.4 = bf16[1,16,128,2,128]{4,1,3,2,0:T(8,128)(2,1)S(1)} collective-permute-done((bf16[1,16,128,2,128]{4,1,3,2,0:T(8,128)(2,1)S(1)}, bf16[1,16,128,2,128]{4,1,3,2,0:T(8,128)(2,1)S(1)}, u32[]{:S(2)}, u32[]{:S(2)}) %collective-permute-start.4) | collective-permute-done | bytes 1048608 | tf_op jit(solution)/shard_map/ppermute | solution.py:15
  368.5 4.9 collective-permute-start.6
  373.5 9.9 %collective-permute-start.7 = (bf16[4,16,128,1,128]{4,1,3,2,0:T(8,128)(2,1)}, bf16[4,16,128,1,128]{4,1,3,2,0:T(8,128)(2,1)}, u32[]{:S(2)}, u32[]{:S(2)}) collective-permute-start(bf16[4,16,128,1,128]{4,1,3,2,0:T(8,128)(2,1)} %get-tuple-element.220), channel_id=1, source_target_pairs={{1,0},{2,1},{3,2},{4,3},{5,4},{6,5},{7,6},{8,7},{9,8},{10,9},{11,1... | collective-permute-start | bytes 6291464 | tf_op jit(solution)/shard_map/ppermute | solution.py:17
  384.0 39.5 %collective-permute-done.6 = bf16[4,16,128,1,128]{4,1,3,2,0:T(8,128)(2,1)} collective-permute-done((bf16[4,16,128,1,128]{4,1,3,2,0:T(8,128)(2,1)}, bf16[4,16,128,1,128]{4,1,3,2,0:T(8,128)(2,1)}, u32[]{:S(2)}, u32[]{:S(2)}) %collective-permute-start.6) | collective-permute-done | bytes 2097184 | tf_op jit(solution)/shard_map/ppermute | solution.py:15
  423.5 86.5 %collective-permute-done.7 = bf16[4,16,128,1,128]{4,1,3,2,0:T(8,128)(2,1)} collective-permute-done((bf16[4,16,128,1,128]{4,1,3,2,0:T(8,128)(2,1)}, bf16[4,16,128,1,128]{4,1,3,2,0:T(8,128)(2,1)}, u32[]{:S(2)}, u32[]{:S(2)}) %collective-permute-start.7) | collective-permute-done | bytes 2097184 | tf_op jit(solution)/shard_map/ppermute | solution.py:17
  510.0 22.6 %select_maximum_fusion = bf16[4,16,130,4,130]{4,1,3,2,0:T(8,128)(2,1)} fusion(bf16[4,16,128,1,128]{4,1,3,2,0:T(8,128)(2,1)} %collective-permute-done.7, bf16[4,16,128,1,128]{4,1,3,2,0:T(8,128)(2,1)} %collective-permute-done.6, bf16[1,16,128,2,128]{4,1,3,2,0:T(8,128)(2,1)} %copy-done, bf16[2,16,128,2,128]{4,1,3,2,0:T(8,128)(2,1)S(1)} %get-tuple-element.103, ...), kind=kLoop, calls=%fused_computation.165 | loop fusion | flops 116812800 | bytes 17041408 | tf_op jit(solution)/shard_map/concatenate | solution.py:13
  532.6 168.0 %while.25 = (s32[]{:T(128)}, f32[2,128,2,128]{3,2,1,0:T(2,128)S(1)}, s32[2]{0:T(128)S(1)}, bf16[4,16,130,4,130]{4,1,3,2,0:T(8,128)(2,1)}, bf16[16,81]{1,0:T(8,128)(2,1)S(1)}) while((s32[]{:T(128)}, f32[2,128,2,128]{3,2,1,0:T(2,128)S(1)}, s32[2]{0:T(128)S(1)}, bf16[4,16,130,4,130]{4,1,3,2,0:T(8,128)(2,1)}, ...), condition=%wide.region_5.6_spmd.clone, body=%wide.region_4.5_spmd.sunk.clone | while | flops 177840640 | bytes 45699956 | solution.py:101
  534.5 10.6 %convolution_bitcast_fusion.10 = f32[27,130,4,130]{3,0,2,1:T(8,128)} fusion(bf16[4,16,130,4,130]{4,1,3,2,0:T(8,128)(2,1)} %get-tuple-element.604, s32[]{:T(128)S(6)} %select_n.32, bf16[16,81]{1,0:T(8,128)(2,1)S(1)} %get-tuple-element.605), kind=kOutput, calls=%fused_computation.60.clone.1.clone | convolution fusion | flops 58406400 | bytes 11563236 | tf_op jit(solution)/shard_map/while/body/eval_jaxpr/dot_general | solution.py:81
  546.4 10.5 %convolution_bitcast_fusion.9 = f32[27,130,4,130]{3,0,2,1:T(8,128)} fusion(bf16[4,16,130,4,130]{4,1,3,2,0:T(8,128)(2,1)} %get-tuple-element.604, s32[]{:T(128)S(6)} %select_n.31, bf16[16,81]{1,0:T(8,128)(2,1)S(1)} %get-tuple-element.605), kind=kOutput, calls=%fused_computation.59.clone.1.clone | convolution fusion | flops 58406400 | bytes 11563236 | tf_op jit(solution)/shard_map/while/body/eval_jaxpr/dot_general | solution.py:81
  558.8 10.4 %convolution_bitcast_fusion.11 = f32[27,130,4,130]{3,0,2,1:T(8,128)} fusion(bf16[4,16,130,4,130]{4,1,3,2,0:T(8,128)(2,1)} %get-tuple-element.604, s32[]{:T(128)S(6)} %select_n.33, bf16[16,81]{1,0:T(8,128)(2,1)S(1)} %get-tuple-element.605), kind=kOutput, calls=%fused_computation.61.clone.1.clone | convolution fusion | flops 58406400 | bytes 11563236 | tf_op jit(solution)/shard_map/while/body/eval_jaxpr/dot_general | solution.py:81
  569.2 47.3 %slice_add_fusion.82 = f32[1,128,2,128]{3,0,2,1:T(1,128)S(1)} fusion(f32[27,130,4,130]{3,0,2,1:T(8,128)} %convolution_bitcast_fusion.9, f32[27,130,4,130]{3,0,2,1:T(8,128)} %convolution_bitcast_fusion.10, f32[27,130,4,130]{3,0,2,1:T(8,128)} %convolution_bitcast_fusion.11), kind=kLoop, calls=%fused_computation.68.clone.1.clone | loop fusion | flops 2621440 | bytes 10747904 | tf_op jit(solution)/shard_map/while/body/eval_jaxpr/add | solution.py:91
  618.5 10.6 %convolution_bitcast_fusion.10 = f32[27,130,4,130]{3,0,2,1:T(8,128)} fusion(bf16[4,16,130,4,130]{4,1,3,2,0:T(8,128)(2,1)} %get-tuple-element.604, s32[]{:T(128)S(6)} %select_n.32, bf16[16,81]{1,0:T(8,128)(2,1)S(1)} %get-tuple-element.605), kind=kOutput, calls=%fused_computation.60.clone.1.clone | convolution fusion | flops 58406400 | bytes 11563236 | tf_op jit(solution)/shard_map/while/body/eval_jaxpr/dot_general | solution.py:81
  630.4 10.5 %convolution_bitcast_fusion.9 = f32[27,130,4,130]{3,0,2,1:T(8,128)} fusion(bf16[4,16,130,4,130]{4,1,3,2,0:T(8,128)(2,1)} %get-tuple-element.604, s32[]{:T(128)S(6)} %select_n.31, bf16[16,81]{1,0:T(8,128)(2,1)S(1)} %get-tuple-element.605), kind=kOutput, calls=%fused_computation.59.clone.1.clone | convolution fusion | flops 58406400 | bytes 11563236 | tf_op jit(solution)/shard_map/while/body/eval_jaxpr/dot_general | solution.py:81
  642.8 10.4 %convolution_bitcast_fusion.11 = f32[27,130,4,130]{3,0,2,1:T(8,128)} fusion(bf16[4,16,130,4,130]{4,1,3,2,0:T(8,128)(2,1)} %get-tuple-element.604, s32[]{:T(128)S(6)} %select_n.33, bf16[16,81]{1,0:T(8,128)(2,1)S(1)} %get-tuple-element.605), kind=kOutput, calls=%fused_computation.61.clone.1.clone | convolution fusion | flops 58406400 | bytes 11563236 | tf_op jit(solution)/shard_map/while/body/eval_jaxpr/dot_general | solution.py:81
  653.2 47.3 %slice_add_fusion.82 = f32[1,128,2,128]{3,0,2,1:T(1,128)S(1)} fusion(f32[27,130,4,130]{3,0,2,1:T(8,128)} %convolution_bitcast_fusion.9, f32[27,130,4,130]{3,0,2,1:T(8,128)} %convolution_bitcast_fusion.10, f32[27,130,4,130]{3,0,2,1:T(8,128)} %convolution_bitcast_fusion.11), kind=kLoop, calls=%fused_computation.68.clone.1.clone | loop fusion | flops 2621440 | bytes 10747904 | tf_op jit(solution)/shard_map/while/body/eval_jaxpr/add | solution.py:91
  (208 shorter events, 161.2 us)
Async XLA Ops:
  0.0 100.3 %copy-start.3 = (bf16[16,81]{1,0:T(8,128)(2,1)S(1)}, bf16[16,81]{1,0:T(8,128)(2,1)}, u32[]{:S(2)}) copy-start(bf16[16,81]{1,0:T(8,128)(2,1)} %param.12) | copy-start | bytes 7780
  0.0 100.3 %copy-start.4 = (f32[16]{0:T(128)S(1)}, f32[16]{0:T(128)}, u32[]{:S(2)}) copy-start(f32[16]{0:T(128)} %param.13) | copy-start | bytes 196
  67.9 12.0 %collective-permute-start = (bf16[1,128,2,128]{3,1,2,0:T(8,128)(2,1)S(1)}, bf16[1,128,2,128]{3,1,2,0:T(8,128)(2,1)S(1)}, u32[]{:S(2)}, u32[]{:S(2)}) collective-permute-start(bf16[1,128,2,128]{3,1,2,0:T(8,128)(2,1)S(1)} %get-tuple-element.225), channel_id=1, source_target_pairs={{0,16},{16,32},{32,48},{48,64},{64,80},{80,96},{96,112},{112,128},... | collective-permute-start | bytes 196616 | tf_op jit(solution)/shard_map/ppermute | solution.py:15
  70.2 11.6 %collective-permute-start.1 = (bf16[1,128,2,128]{3,1,2,0:T(8,128)(2,1)S(1)}, bf16[1,128,2,128]{3,1,2,0:T(8,128)(2,1)S(1)}, u32[]{:S(2)}, u32[]{:S(2)}) collective-permute-start(bf16[1,128,2,128]{3,1,2,0:T(8,128)(2,1)S(1)} %get-tuple-element.226), channel_id=1, source_target_pairs={{16,0},{32,16},{48,32},{64,48},{80,64},{96,80},{112,96},{128,112},... | collective-permute-start | bytes 196616 | tf_op jit(solution)/shard_map/ppermute | solution.py:17
  81.8 8.2 %collective-permute-start.2 = (bf16[4,128,1,128]{3,1,2,0:T(8,128)(2,1)S(1)}, bf16[4,128,1,128]{3,1,2,0:T(8,128)(2,1)S(1)}, u32[]{:S(2)}, u32[]{:S(2)}) collective-permute-start(bf16[4,128,1,128]{3,1,2,0:T(8,128)(2,1)S(1)} %get-tuple-element.223), channel_id=1, source_target_pairs={{0,1},{1,2},{2,3},{3,4},{4,5},{5,6},{6,7},{7,8},{8,9},{9,10},{10,1... | collective-permute-start | bytes 393224 | tf_op jit(solution)/shard_map/ppermute | solution.py:15
  87.5 11.0 %collective-permute-start.3 = (bf16[4,128,1,128]{3,1,2,0:T(8,128)(2,1)S(1)}, bf16[4,128,1,128]{3,1,2,0:T(8,128)(2,1)}, u32[]{:S(2)}, u32[]{:S(2)}) collective-permute-start(bf16[4,128,1,128]{3,1,2,0:T(8,128)(2,1)S(1)} %get-tuple-element.224), channel_id=1, source_target_pairs={{1,0},{2,1},{3,2},{4,3},{5,4},{6,5},{7,6},{8,7},{9,8},{10,9},{11,1... | collective-permute-start | bytes 393224 | tf_op jit(solution)/shard_map/ppermute | solution.py:17
  90.0 0.7 copy-start.2
  326.0 38.3 %collective-permute-start.4 = (bf16[1,16,128,2,128]{4,1,3,2,0:T(8,128)(2,1)S(1)}, bf16[1,16,128,2,128]{4,1,3,2,0:T(8,128)(2,1)S(1)}, u32[]{:S(2)}, u32[]{:S(2)}) collective-permute-start(bf16[1,16,128,2,128]{4,1,3,2,0:T(8,128)(2,1)S(1)} %get-tuple-element.221), channel_id=1, source_target_pairs={{0,16},{16,32},{32,48},{48,64},{64,80},{80,96},{96,112},{112,128},... | collective-permute-start | bytes 3145736 | tf_op jit(solution)/shard_map/ppermute | solution.py:15
  329.8 34.5 %collective-permute-start.5 = (bf16[1,16,128,2,128]{4,1,3,2,0:T(8,128)(2,1)S(1)}, bf16[1,16,128,2,128]{4,1,3,2,0:T(8,128)(2,1)S(1)}, u32[]{:S(2)}, u32[]{:S(2)}) collective-permute-start(bf16[1,16,128,2,128]{4,1,3,2,0:T(8,128)(2,1)S(1)} %get-tuple-element.222), channel_id=1, source_target_pairs={{16,0},{32,16},{48,32},{64,48},{80,64},{96,80},{112,96},{128,112},... | collective-permute-start | bytes 3145736 | tf_op jit(solution)/shard_map/ppermute | solution.py:17
  364.3 1.0 copy-start
  368.5 55.0 %collective-permute-start.6 = (bf16[4,16,128,1,128]{4,1,3,2,0:T(8,128)(2,1)}, bf16[4,16,128,1,128]{4,1,3,2,0:T(8,128)(2,1)}, u32[]{:S(2)}, u32[]{:S(2)}) collective-permute-start(bf16[4,16,128,1,128]{4,1,3,2,0:T(8,128)(2,1)} %get-tuple-element.219), channel_id=1, source_target_pairs={{0,1},{1,2},{2,3},{3,4},{4,5},{5,6},{6,7},{7,8},{8,9},{9,10},{10,1... | collective-permute-start | bytes 6291464 | tf_op jit(solution)/shard_map/ppermute | solution.py:15
  373.5 136.6 %collective-permute-start.7 = (bf16[4,16,128,1,128]{4,1,3,2,0:T(8,128)(2,1)}, bf16[4,16,128,1,128]{4,1,3,2,0:T(8,128)(2,1)}, u32[]{:S(2)}, u32[]{:S(2)}) collective-permute-start(bf16[4,16,128,1,128]{4,1,3,2,0:T(8,128)(2,1)} %get-tuple-element.220), channel_id=1, source_target_pairs={{1,0},{2,1},{3,2},{4,3},{5,4},{6,5},{7,6},{8,7},{9,8},{10,9},{11,1... | collective-permute-start | bytes 6291464 | tf_op jit(solution)/shard_map/ppermute | solution.py:17
  384.0 148.6 %copy-start.1 = (bf16[16,81]{1,0:T(8,128)(2,1)S(1)}, bf16[16,81]{1,0:T(8,128)(2,1)}, u32[]{:S(2)}) copy-start(bf16[16,81]{1,0:T(8,128)(2,1)} %param.14) | copy-start | bytes 7780
where the time goes:
time: 708 us; the launch traced here: 701 us
  local copies, waits for them, and re-layouts  220 us (31%)
  waiting for transfers between devices  165 us (23%)
  other arithmetic  124 us (18%)
  matrix products  70.7 us (10%)
  blocking collectives  64.1 us (9%)
  starting transfers between devices  43.8 us (6%)
  loops' own time  13.4 us (2%)
    while x162, local copies, waits for them, and re-layouts  120 us
    ppermute x4, waiting for transfers between devices, extended(): lax.ppermute(head, axis, [((i + 1) % count, i) for i in range(ends)])  96.3 us
    add x2, other arithmetic, second_one_row(): total + taps[9 * t_j + 3 * t_k + t_l, t_j:t_j + width_j, t_k:t_k + out_k,...  94.6 us
    another operation x2, local copies, waits for them, and re-layouts, first_one_row(): jnp.stack([block[t_i, t_j:t_j + width_j, t_k:t_k + out_k, t_l:t_l + width...  83.1 us
    ppermute x4, waiting for transfers between devices, extended(): lax.ppermute(tail, axis, [(i, (i + 1) % count) for i in range(ends)])  68.9 us
    dot_general x6, matrix products, second_one_row(): lax.dot_general(weight_two[:, 27 * t_i:27 * t_i + 27], plane, (((0,), (0,...  63 us
    all_gather x1, blocking collectives, correlate(): gathered = lax.all_gather(norm_a, 'rb', axis=1, tiled=True)  36.8 us
    all_gather x1, blocking collectives, correlate(): piece = lax.all_gather(norm_b, 'ra', axis=1, tiled=True)  27.3 us
  transfers between devices with their start and end apart: 8, of which 6 were waited for; matrix products, arithmetic and copies ran while one was open for 0% of the time, Pallas kernels for 0%

commit v1 on v0

--- a/solution.py
+++ b/solution.py
@@ -28,7 +28,10 @@
 
 
 def correlate(norm_a, norm_b):
-    gathered = lax.all_gather(norm_a, "rb", axis=1, tiled=True)
+    size = lax.axis_size("rb")
+    blocks = jnp.stack([norm_a for _ in range(size)])
+    blocks = lax.all_to_all(blocks, "rb", split_axis=0, concat_axis=0)
+    gathered = jnp.concatenate(blocks, axis=1)
     channels = gathered.shape[2]
     flat_a = gathered.reshape(-1, channels)
     piece = lax.all_gather(norm_b, "ra", axis=1, tiled=True)

time: 708 us -> 651 us (0.919)
  the two profiles are of different devices: /device:TPU:232 before, /device:TPU:39 now
where the time goes in v1:
time: 651 us; the launch traced here: 644 us
  local copies, waits for them, and re-layouts  221 us (34%)
  waiting for transfers between devices  146 us (22%)
  other arithmetic  126 us (19%)
  matrix products  70.7 us (11%)
  starting transfers between devices  35 us (5%)
  blocking collectives  31.7 us (5%)
  loops' own time  13.4 us (2%)
    while x162, local copies, waits for them, and re-layouts  120 us
    add x2, other arithmetic, second_one_row(): total + taps[9 * t_j + 3 * t_k + t_l, t_j:t_j + width_j, t_k:t_k + out_k,...  96.7 us
    another operation x2, local copies, waits for them, and re-layouts, first_one_row(): jnp.stack([block[t_i, t_j:t_j + width_j, t_k:t_k + out_k, t_l:t_l + width...  83.1 us
    ppermute x4, waiting for transfers between devices, extended(): lax.ppermute(tail, axis, [(i, (i + 1) % count) for i in range(ends)])  80.2 us
    ppermute x4, waiting for transfers between devices, extended(): lax.ppermute(head, axis, [((i + 1) % count, i) for i in range(ends)])  66.1 us
    dot_general x6, matrix products, second_one_row(): lax.dot_general(weight_two[:, 27 * t_i:27 * t_i + 27], plane, (((0,), (0,...  63 us
    all_gather x1, blocking collectives, correlate(): piece = lax.all_gather(norm_b, 'ra', axis=1, tiled=True)  31.7 us
    concatenate x4, other arithmetic, extended(): jnp.concatenate([lax.ppermute(tail, axis, [(i, (i + 1) % count) for i in...  24.9 us
  transfers between devices with their start and end apart: 9, of which 5 were waited for; matrix products, arithmetic and copies ran while one was open for 0% of the time, Pallas kernels for 0%

profile of v1, /device:TPU:39, one launch (start us, length us, event | category | flops | bytes accessed | tf_op | source)
XLA Modules:
  0.0 644.4 jit_solution(11417510354004948233)
XLA Ops:
  2.6 8.1 %all-to-all-start = ((bf16[16,2,8,1024]{3,2,1,0:T(8,128)(2,1)}), bf16[16,2,8,1024]{3,2,1,0:T(8,128)(2,1)S(1)}, u32[]{:S(2)}, u32[]{:S(2)}) async-start(bf16[16,2,8,1024]{3,2,1,0:T(8,128)(2,1)} %stack.4), calls=%async_computation | async-start | bytes 1048576 | tf_op jit(solution)/shard_map/all_to_all | solution.py:33
  12.4 31.7 %all_gather.3 = bf16[2,128,1024]{2,1,0:T(8,128)(2,1)S(1)} all-gather(bf16[2,8,1024]{2,1,0:T(8,128)(2,1)S(1)} %fusion.44), channel_id=1, replica_groups=mesh['ra'=16,'rb'=16] {'ra'}, dimensions={1}, use_global_device_ids=true | all-gather | bytes 557056 | tf_op jit(solution)/shard_map/all_gather | solution.py:37
  49.7 7.6 %collective-permute-done.1 = bf16[1,128,2,128]{3,1,2,0:T(8,128)(2,1)S(1)} collective-permute-done((bf16[1,128,2,128]{3,1,2,0:T(8,128)(2,1)S(1)}, bf16[1,128,2,128]{3,1,2,0:T(8,128)(2,1)S(1)}, u32[]{:S(2)}, u32[]{:S(2)}) %collective-permute-start.1) | collective-permute-done | bytes 65568 | tf_op jit(solution)/shard_map/ppermute | solution.py:17
  57.3 6.2 collective-permute-start.2
  66.2 4.9 collective-permute-done.3
  72.9 225.3 %while.24 = (s32[]{:T(128)}, bf16[2,16,128,2,128]{4,1,3,2,0:T(8,128)(2,1)S(1)}, s32[2]{0:T(128)S(1)}, bf16[4,130,4,130]{3,1,2,0:T(8,128)(2,1)S(1)}, bf16[16,81]{1,0:T(8,128)(2,1)S(1)}, /*index=5*/f32[16]{0:T(128)S(1)}) while((s32[]{:T(128)}, bf16[2,16,128,2,128]{4,1,3,2,0:T(8,128)(2,1)S(1)}, s32[2]{0:T(128)S(1)}, ...), condition=%wide.region_3.4_spmd.clone, body=%wide.region_2.3_spmd.sunk.clone | while | flops 85983240 | bytes 39260856 | solution.py:73
  75.5 4.8 fusion.72
  140.2 41.6 %stack.7 = bf16[81,128,2,128]{3,0,2,1:T(8,128)(2,1)} concatenate(bf16[1,128,2,128]{3,0,2,1:T(2,128)(2,1)S(1)} %copy.271, bf16[1,128,2,128]{3,0,2,1:T(2,128)(2,1)S(1)} %copy.272, bf16[1,128,2,128]{3,0,2,1:T(2,128)(2,1)} %copy.273, bf16[1,128,2,128]{3,0,2,1:T(2,128)(2,1)} %copy.274, bf16[1,128,2,128]{3,0,2,1:T(2,128)(2,1)} %copy.275, bf16[1,128,2,128]{3,0,2,1:T(2,128)(2,1)} %copy.276, ...), dimensions={0} | concatenate | bytes 10616832 | tf_op jit(solution)/shard_map/while/body/eval_jaxpr/stack | solution.py:59
  188.0 4.8 fusion.72
  252.8 41.6 %stack.7 = bf16[81,128,2,128]{3,0,2,1:T(8,128)(2,1)} concatenate(bf16[1,128,2,128]{3,0,2,1:T(2,128)(2,1)S(1)} %copy.271, bf16[1,128,2,128]{3,0,2,1:T(2,128)(2,1)S(1)} %copy.272, bf16[1,128,2,128]{3,0,2,1:T(2,128)(2,1)} %copy.273, bf16[1,128,2,128]{3,0,2,1:T(2,128)(2,1)} %copy.274, bf16[1,128,2,128]{3,0,2,1:T(2,128)(2,1)} %copy.275, bf16[1,128,2,128]{3,0,2,1:T(2,128)(2,1)} %copy.276, ...), dimensions={0} | concatenate | bytes 10616832 | tf_op jit(solution)/shard_map/while/body/eval_jaxpr/stack | solution.py:59
  303.1 39.0 %collective-permute-done.4 = bf16[1,16,128,2,128]{4,1,3,2,0:T(8,128)(2,1)S(1)} collective-permute-done((bf16[1,16,128,2,128]{4,1,3,2,0:T(8,128)(2,1)S(1)}, bf16[1,16,128,2,128]{4,1,3,2,0:T(8,128)(2,1)S(1)}, u32[]{:S(2)}, u32[]{:S(2)}) %collective-permute-start.4) | collective-permute-done | bytes 1048608 | tf_op jit(solution)/shard_map/ppermute | solution.py:15
  346.4 7.2 %collective-permute-start.6 = (bf16[4,16,128,1,128]{4,1,3,2,0:T(8,128)(2,1)}, bf16[4,16,128,1,128]{4,1,3,2,0:T(8,128)(2,1)}, u32[]{:S(2)}, u32[]{:S(2)}) collective-permute-start(bf16[4,16,128,1,128]{4,1,3,2,0:T(8,128)(2,1)} %get-tuple-element.230), channel_id=1, source_target_pairs={{0,1},{1,2},{2,3},{3,4},{4,5},{5,6},{6,7},{7,8},{8,9},{9,10},{10,1... | collective-permute-start | bytes 6291464 | tf_op jit(solution)/shard_map/ppermute | solution.py:15
  356.2 41.2 %collective-permute-done.6 = bf16[4,16,128,1,128]{4,1,3,2,0:T(8,128)(2,1)} collective-permute-done((bf16[4,16,128,1,128]{4,1,3,2,0:T(8,128)(2,1)}, bf16[4,16,128,1,128]{4,1,3,2,0:T(8,128)(2,1)}, u32[]{:S(2)}, u32[]{:S(2)}) %collective-permute-start.6) | collective-permute-done | bytes 2097184 | tf_op jit(solution)/shard_map/ppermute | solution.py:15
  397.4 53.6 %collective-permute-done.7 = bf16[4,16,128,1,128]{4,1,3,2,0:T(8,128)(2,1)} collective-permute-done((bf16[4,16,128,1,128]{4,1,3,2,0:T(8,128)(2,1)}, bf16[4,16,128,1,128]{4,1,3,2,0:T(8,128)(2,1)}, u32[]{:S(2)}, u32[]{:S(2)}) %collective-permute-start.7) | collective-permute-done | bytes 2097184 | tf_op jit(solution)/shard_map/ppermute | solution.py:17
  450.9 22.6 %select_maximum_fusion = bf16[4,16,130,4,130]{4,1,3,2,0:T(8,128)(2,1)} fusion(bf16[4,16,128,1,128]{4,1,3,2,0:T(8,128)(2,1)} %collective-permute-done.7, bf16[4,16,128,1,128]{4,1,3,2,0:T(8,128)(2,1)} %collective-permute-done.6, bf16[1,16,128,2,128]{4,1,3,2,0:T(8,128)(2,1)} %copy-done, bf16[2,16,128,2,128]{4,1,3,2,0:T(8,128)(2,1)S(1)} %get-tuple-element.103, ...), kind=kLoop, calls=%fused_computation.165 | loop fusion | flops 116812800 | bytes 17041408 | tf_op jit(solution)/shard_map/concatenate | solution.py:13
  473.5 170.0 %while.25 = (s32[]{:T(128)}, f32[2,128,2,128]{3,2,1,0:T(2,128)S(1)}, s32[2]{0:T(128)S(1)}, bf16[4,16,130,4,130]{4,1,3,2,0:T(8,128)(2,1)}, bf16[16,81]{1,0:T(8,128)(2,1)S(1)}) while((s32[]{:T(128)}, f32[2,128,2,128]{3,2,1,0:T(2,128)S(1)}, s32[2]{0:T(128)S(1)}, bf16[4,16,130,4,130]{4,1,3,2,0:T(8,128)(2,1)}, ...), condition=%wide.region_5.6_spmd.clone, body=%wide.region_4.5_spmd.sunk.clone | while | flops 177840640 | bytes 45699956 | solution.py:104
  475.4 10.5 %convolution_bitcast_fusion.10 = f32[27,130,4,130]{3,0,2,1:T(8,128)} fusion(bf16[4,16,130,4,130]{4,1,3,2,0:T(8,128)(2,1)} %get-tuple-element.615, s32[]{:T(128)S(6)} %select_n.32, bf16[16,81]{1,0:T(8,128)(2,1)S(1)} %get-tuple-element.616), kind=kOutput, calls=%fused_computation.60.clone.1.clone | convolution fusion | flops 58406400 | bytes 11563236 | tf_op jit(solution)/shard_map/while/body/eval_jaxpr/dot_general | solution.py:84
  487.3 10.5 %convolution_bitcast_fusion.9 = f32[27,130,4,130]{3,0,2,1:T(8,128)} fusion(bf16[4,16,130,4,130]{4,1,3,2,0:T(8,128)(2,1)} %get-tuple-element.615, s32[]{:T(128)S(6)} %select_n.31, bf16[16,81]{1,0:T(8,128)(2,1)S(1)} %get-tuple-element.616), kind=kOutput, calls=%fused_computation.59.clone.1.clone | convolution fusion | flops 58406400 | bytes 11563236 | tf_op jit(solution)/shard_map/while/body/eval_jaxpr/dot_general | solution.py:84
  499.7 10.4 %convolution_bitcast_fusion.11 = f32[27,130,4,130]{3,0,2,1:T(8,128)} fusion(bf16[4,16,130,4,130]{4,1,3,2,0:T(8,128)(2,1)} %get-tuple-element.615, s32[]{:T(128)S(6)} %select_n.33, bf16[16,81]{1,0:T(8,128)(2,1)S(1)} %get-tuple-element.616), kind=kOutput, calls=%fused_computation.61.clone.1.clone | convolution fusion | flops 58406400 | bytes 11563236 | tf_op jit(solution)/shard_map/while/body/eval_jaxpr/dot_general | solution.py:84
  510.1 48.3 %slice_add_fusion.82 = f32[1,128,2,128]{3,0,2,1:T(1,128)S(1)} fusion(f32[27,130,4,130]{3,0,2,1:T(8,128)} %convolution_bitcast_fusion.9, f32[27,130,4,130]{3,0,2,1:T(8,128)} %convolution_bitcast_fusion.10, f32[27,130,4,130]{3,0,2,1:T(8,128)} %convolution_bitcast_fusion.11), kind=kLoop, calls=%fused_computation.68.clone.1.clone | loop fusion | flops 2621440 | bytes 10747904 | tf_op jit(solution)/shard_map/while/body/eval_jaxpr/add | solution.py:94
  560.4 10.5 %convolution_bitcast_fusion.10 = f32[27,130,4,130]{3,0,2,1:T(8,128)} fusion(bf16[4,16,130,4,130]{4,1,3,2,0:T(8,128)(2,1)} %get-tuple-element.615, s32[]{:T(128)S(6)} %select_n.32, bf16[16,81]{1,0:T(8,128)(2,1)S(1)} %get-tuple-element.616), kind=kOutput, calls=%fused_computation.60.clone.1.clone | convolution fusion | flops 58406400 | bytes 11563236 | tf_op jit(solution)/shard_map/while/body/eval_jaxpr/dot_general | solution.py:84
  572.3 10.5 %convolution_bitcast_fusion.9 = f32[27,130,4,130]{3,0,2,1:T(8,128)} fusion(bf16[4,16,130,4,130]{4,1,3,2,0:T(8,128)(2,1)} %get-tuple-element.615, s32[]{:T(128)S(6)} %select_n.31, bf16[16,81]{1,0:T(8,128)(2,1)S(1)} %get-tuple-element.616), kind=kOutput, calls=%fused_computation.59.clone.1.clone | convolution fusion | flops 58406400 | bytes 11563236 | tf_op jit(solution)/shard_map/while/body/eval_jaxpr/dot_general | solution.py:84
  584.7 10.4 %convolution_bitcast_fusion.11 = f32[27,130,4,130]{3,0,2,1:T(8,128)} fusion(bf16[4,16,130,4,130]{4,1,3,2,0:T(8,128)(2,1)} %get-tuple-element.615, s32[]{:T(128)S(6)} %select_n.33, bf16[16,81]{1,0:T(8,128)(2,1)S(1)} %get-tuple-element.616), kind=kOutput, calls=%fused_computation.61.clone.1.clone | convolution fusion | flops 58406400 | bytes 11563236 | tf_op jit(solution)/shard_map/while/body/eval_jaxpr/dot_general | solution.py:84
  595.1 48.3 %slice_add_fusion.82 = f32[1,128,2,128]{3,0,2,1:T(1,128)S(1)} fusion(f32[27,130,4,130]{3,0,2,1:T(8,128)} %convolution_bitcast_fusion.9, f32[27,130,4,130]{3,0,2,1:T(8,128)} %convolution_bitcast_fusion.10, f32[27,130,4,130]{3,0,2,1:T(8,128)} %convolution_bitcast_fusion.11), kind=kLoop, calls=%fused_computation.68.clone.1.clone | loop fusion | flops 2621440 | bytes 10747904 | tf_op jit(solution)/shard_map/while/body/eval_jaxpr/add | solution.py:94
  (210 shorter events, 155.7 us)
Async XLA Ops:
  0.0 72.9 %copy-start.3 = (bf16[16,81]{1,0:T(8,128)(2,1)S(1)}, bf16[16,81]{1,0:T(8,128)(2,1)}, u32[]{:S(2)}) copy-start(bf16[16,81]{1,0:T(8,128)(2,1)} %param.12) | copy-start | bytes 7780
  0.0 72.9 %copy-start.4 = (f32[16]{0:T(128)S(1)}, f32[16]{0:T(128)}, u32[]{:S(2)}) copy-start(f32[16]{0:T(128)} %param.13) | copy-start | bytes 196
  2.6 41.5 %all-to-all-start = ((bf16[16,2,8,1024]{3,2,1,0:T(8,128)(2,1)}), bf16[16,2,8,1024]{3,2,1,0:T(8,128)(2,1)S(1)}, u32[]{:S(2)}, u32[]{:S(2)}) async-start(bf16[16,2,8,1024]{3,2,1,0:T(8,128)(2,1)} %stack.4), calls=%async_computation | async-start | bytes 1048576 | tf_op jit(solution)/shard_map/all_to_all | solution.py:33
  44.5 5.2 collective-permute-start
  47.8 9.5 %collective-permute-start.1 = (bf16[1,128,2,128]{3,1,2,0:T(8,128)(2,1)S(1)}, bf16[1,128,2,128]{3,1,2,0:T(8,128)(2,1)S(1)}, u32[]{:S(2)}, u32[]{:S(2)}) collective-permute-start(bf16[1,128,2,128]{3,1,2,0:T(8,128)(2,1)S(1)} %get-tuple-element.237), channel_id=1, source_target_pairs={{16,0},{32,16},{48,32},{64,48},{80,64},{96,80},{112,96},{128,112},... | collective-permute-start | bytes 196616 | tf_op jit(solution)/shard_map/ppermute | solution.py:17
  57.3 8.2 %collective-permute-start.2 = (bf16[4,128,1,128]{3,1,2,0:T(8,128)(2,1)S(1)}, bf16[4,128,1,128]{3,1,2,0:T(8,128)(2,1)S(1)}, u32[]{:S(2)}, u32[]{:S(2)}) collective-permute-start(bf16[4,128,1,128]{3,1,2,0:T(8,128)(2,1)S(1)} %get-tuple-element.234), channel_id=1, source_target_pairs={{0,1},{1,2},{2,3},{3,4},{4,5},{5,6},{6,7},{7,8},{8,9},{9,10},{10,1... | collective-permute-start | bytes 393224 | tf_op jit(solution)/shard_map/ppermute | solution.py:15
  63.6 7.6 %collective-permute-start.3 = (bf16[4,128,1,128]{3,1,2,0:T(8,128)(2,1)S(1)}, bf16[4,128,1,128]{3,1,2,0:T(8,128)(2,1)}, u32[]{:S(2)}, u32[]{:S(2)}) collective-permute-start(bf16[4,128,1,128]{3,1,2,0:T(8,128)(2,1)S(1)} %get-tuple-element.235), channel_id=1, source_target_pairs={{1,0},{2,1},{3,2},{4,3},{5,4},{6,5},{7,6},{8,7},{9,8},{10,9},{11,1... | collective-permute-start | bytes 393224 | tf_op jit(solution)/shard_map/ppermute | solution.py:17
  65.5 0.7 copy-start.2
  298.6 43.5 %collective-permute-start.4 = (bf16[1,16,128,2,128]{4,1,3,2,0:T(8,128)(2,1)S(1)}, bf16[1,16,128,2,128]{4,1,3,2,0:T(8,128)(2,1)S(1)}, u32[]{:S(2)}, u32[]{:S(2)}) collective-permute-start(bf16[1,16,128,2,128]{4,1,3,2,0:T(8,128)(2,1)S(1)} %get-tuple-element.232), channel_id=1, source_target_pairs={{0,16},{16,32},{32,48},{48,64},{64,80},{80,96},{96,112},{112,128},... | collective-permute-start | bytes 3145736 | tf_op jit(solution)/shard_map/ppermute | solution.py:15
  301.2 41.0 %collective-permute-start.5 = (bf16[1,16,128,2,128]{4,1,3,2,0:T(8,128)(2,1)S(1)}, bf16[1,16,128,2,128]{4,1,3,2,0:T(8,128)(2,1)S(1)}, u32[]{:S(2)}, u32[]{:S(2)}) collective-permute-start(bf16[1,16,128,2,128]{4,1,3,2,0:T(8,128)(2,1)S(1)} %get-tuple-element.233), channel_id=1, source_target_pairs={{16,0},{32,16},{48,32},{64,48},{80,64},{96,80},{112,96},{128,112},... | collective-permute-start | bytes 3145736 | tf_op jit(solution)/shard_map/ppermute | solution.py:17
  342.2 1.0 copy-start
  346.4 50.9 %collective-permute-start.6 = (bf16[4,16,128,1,128]{4,1,3,2,0:T(8,128)(2,1)}, bf16[4,16,128,1,128]{4,1,3,2,0:T(8,128)(2,1)}, u32[]{:S(2)}, u32[]{:S(2)}) collective-permute-start(bf16[4,16,128,1,128]{4,1,3,2,0:T(8,128)(2,1)} %get-tuple-element.230), channel_id=1, source_target_pairs={{0,1},{1,2},{2,3},{3,4},{4,5},{5,6},{6,7},{7,8},{8,9},{9,10},{10,1... | collective-permute-start | bytes 6291464 | tf_op jit(solution)/shard_map/ppermute | solution.py:15
  353.6 97.3 %collective-permute-start.7 = (bf16[4,16,128,1,128]{4,1,3,2,0:T(8,128)(2,1)}, bf16[4,16,128,1,128]{4,1,3,2,0:T(8,128)(2,1)}, u32[]{:S(2)}, u32[]{:S(2)}) collective-permute-start(bf16[4,16,128,1,128]{4,1,3,2,0:T(8,128)(2,1)} %get-tuple-element.231), channel_id=1, source_target_pairs={{1,0},{2,1},{3,2},{4,3},{5,4},{6,5},{7,6},{8,7},{9,8},{10,9},{11,1... | collective-permute-start | bytes 6291464 | tf_op jit(solution)/shard_map/ppermute | solution.py:17
  356.2 117.3 %copy-start.1 = (bf16[16,81]{1,0:T(8,128)(2,1)S(1)}, bf16[16,81]{1,0:T(8,128)(2,1)}, u32[]{:S(2)}) copy-start(bf16[16,81]{1,0:T(8,128)(2,1)} %param.14) | copy-start | bytes 7780
